TPU v7x, 256 devices: a whole 4x4x8 slice. The times are simulated.
256 devices in a mesh: depth: 8 (over x_hi, y), lat: 32 (over z, x_lo, core).
Axes of the slice: x: 4 (x_hi: 2, x_lo: 2; x = x_hi * 2 + x_lo), y: 4, z: 8, core: 2. Of those that a mesh axis runs over, the one named last changes fastest.
Arguments:
- operator: float32 [8, 160, 9, 256, 128], P('depth', 'lat'), may hold values from -0.125 to 0.125
- band_shift: int32 [8, 160], P('depth', 'lat'), may hold values from -1 to 1, as said below
- reflectivity: float32 [8, 20480], P('depth', 'lat'), may hold values from -0.4 to 0.4
- up_stored: float32 [8, 20480, 128], P('depth', 'lat'), may hold values from -6 to 6
- down_stored: float32 [8, 20480, 128], P('depth', 'lat'), may hold values from -6 to 6
- sources: float32 [20480, 128], P('lat'), may hold values from -6 to 6
- assignment: int32 [64], replicated, may hold values from 0 to 63, each once
Outputs:
- down_fields: float32 [8, 20480, 128], P('depth', 'lat')
- up_fields: float32 [8, 20480, 128], P('depth', 'lat')
Inputs may be any that keep to these rules, and one draw needn't show every extreme that they name: `band_shift`: in every section some tile row has -1 and some has +1.
All inputs are finite; a program needn't handle non-finite values.
Results may differ from a plain program's by a relative error of at most 0.00013.
Values sent between devices are 32-bit elements; how exact they have to be, the bound alone decides.
A program may use at most 64 MiB of HBM per device.

v0:
```python
import jax
import jax.numpy as jnp
from jax import lax
from jax.experimental import pallas as pl
from jax.experimental.pallas import tpu as pltpu
from jax.sharding import PartitionSpec as P

TILE = 128
SHOTS = 32
GROUP = 8
ROWS = 2 * GROUP
CHUNKS = 2 * SHOTS // GROUP
PER_BATCH = SHOTS // GROUP
COLS = 4 * SHOTS
DOWN, UP = 0, 1
MESH = pl.DeviceIdType.MESH


def column_group(chunk, part):
    return (chunk // PER_BATCH) * 2 * PER_BATCH + part * PER_BATCH + chunk % PER_BATCH


def kernel(
    sections,
    lat_devices,
    operator,
    shift,
    reflect,
    up_stored,
    down_stored,
    sources,
    assignment,
    down_out,
    up_out,
    raw,
    high,
    low,
    up_rows,
    down_rows,
    source_rows,
    local,
    weight,
    arrived,
    result,
    split,
    load_sem,
    raw_sem,
    local_send,
    local_recv,
    weight_send,
    weight_recv,
    field_send,
    field_recv,
):
    depth = lax.axis_index("depth")
    lat = lax.axis_index("lat")
    tiles = raw.shape[0]
    width = tiles * TILE

    loads = [
        pltpu.make_async_copy(source, target, load_sem.at[n])
        for n, (source, target) in enumerate(
            [
                (sources, source_rows),
                (up_stored.at[0], up_rows),
                (down_stored.at[0], down_rows),
            ]
        )
    ]
    raw_loads = [
        pltpu.make_async_copy(operator.at[0, g], raw.at[g], raw_sem.at[g]) for g in range(tiles)
    ]
    for copy in loads:
        copy.start()
    for copy in raw_loads:
        copy.start()

    def lat_ok(step):
        return (lat + step >= 0) & (lat + step < lat_devices)

    def depth_ok(step):
        return (depth + step >= 0) & (depth + step < sections)

    barrier = pltpu.get_barrier_semaphore()
    greeted = 0
    for down_by in (-1, 0, 1):
        for right_by in (-1, 0, 1):
            if (down_by, right_by) == (0, 0):
                continue
            ok = lat_ok(right_by) & depth_ok(down_by)
            greeted = greeted + ok.astype(jnp.int32)

            @pl.when(ok)
            def _():
                pl.semaphore_signal(
                    barrier,
                    inc=1,
                    device_id=(depth + down_by, lat + right_by),
                    device_id_type=MESH,
                )

    strength = reflect[...]
    weight[1] = jnp.broadcast_to(strength, (8, width))

    def put_local(which, rows, scale, offset=None):
        for g in range(tiles):
            flipped = jnp.transpose(rows[g * TILE : (g + 1) * TILE, :])
            here = slice(g * TILE, (g + 1) * TILE)
            for chunk in range(CHUNKS):
                for part in range(2):
                    group = column_group(chunk, part)
                    value = flipped[group * GROUP : (group + 1) * GROUP] * scale[:, here]
                    if offset is not None:
                        value = value + local[which, chunk, 1, part * GROUP : (part + 1) * GROUP, here]
                    local[which, chunk, 1, part * GROUP : (part + 1) * GROUP, here] = value

    loads[0].wait()
    loads[1].wait()
    put_local(DOWN, up_rows[...], -strength)

    @pl.when(depth == 0)
    def _():
        lanes = lax.broadcasted_iota(jnp.int32, (1, COLS), 1)
        wanted = jnp.zeros((1, COLS), jnp.int32)
        for slot in range(2 * SHOTS):
            column = (slot // SHOTS) * 2 * SHOTS + slot % SHOTS
            wanted = jnp.where(lanes == column, assignment[slot], wanted)
            wanted = jnp.where(lanes == column + SHOTS, assignment[slot] + 2 * SHOTS, wanted)
        chosen = (lax.broadcasted_iota(jnp.int32, (COLS, COLS), 0) == wanted).astype(jnp.float32)
        entering = jnp.dot(
            source_rows[...],
            chosen,
            precision=lax.Precision.HIGHEST,
            preferred_element_type=jnp.float32,
        )
        put_local(DOWN, entering, 1.0 + strength, offset=True)
        arrived[DOWN] = jnp.zeros(arrived.shape[1:], jnp.float32)

    loads[2].wait()
    put_local(UP, down_rows[...], strength)

    @pl.when(depth == sections - 1)
    def _():
        arrived[UP] = jnp.zeros(arrived.shape[1:], jnp.float32)

    for edge, slot in ((0, 0), (lat_devices - 1, 2)):

        @pl.when(lat == edge)
        def _():
            weight[slot] = jnp.zeros(weight.shape[1:], jnp.float32)

            def clear(which, _):
                for chunk in range(CHUNKS):
                    local[which, chunk, slot] = jnp.zeros((ROWS, width), jnp.float32)
                    arrived[which, chunk, slot] = jnp.zeros((ROWS, width), jnp.float32)
                return 0

            lax.fori_loop(0, 2, clear, 0)

    pl.semaphore_wait(barrier, greeted)

    def weight_copy(step):
        slot = 1 - step
        return pltpu.make_async_remote_copy(
            src_ref=weight.at[1],
            dst_ref=weight.at[slot],
            send_sem=weight_send.at[slot],
            recv_sem=weight_recv.at[slot],
            device_id=(depth, lat + step),
            device_id_type=MESH,
        )

    def local_copy(which, chunk, step):
        slot = 1 - step
        return pltpu.make_async_remote_copy(
            src_ref=local.at[which, chunk, 1],
            dst_ref=local.at[which, chunk, slot],
            send_sem=local_send.at[which, chunk, slot],
            recv_sem=local_recv.at[which, chunk, slot],
            device_id=(depth, lat + step),
            device_id_type=MESH,
        )

    def field_copy(which, chunk, step):
        slot = 1 - step
        return pltpu.make_async_remote_copy(
            src_ref=result.at[which, chunk],
            dst_ref=arrived.at[which, chunk, slot],
            send_sem=field_send.at[which, chunk, slot],
            recv_sem=field_recv.at[which, chunk, slot],
            device_id=(depth + 1 - 2 * which, lat + step),
            device_id_type=MESH,
        )

    early = jnp.where(2 * depth < sections, DOWN, UP)
    lag = jnp.where((depth == sections // 2 - 1) | (depth == sections // 2), 3, CHUNKS)

    def event(number):
        mixed = (number >= lag) & (number < 2 * CHUNKS - lag)
        turn = (number - lag) // 2
        odd = (number - lag) % 2
        of_early = (number < lag) | (mixed & (odd == 1))
        chunk = jnp.where(
            number < lag,
            number,
            jnp.where(mixed, jnp.where(odd == 1, lag + turn, turn), number - CHUNKS),
        )
        return jnp.where(of_early, early, 1 - early), chunk

    for step in (-1, 1):

        @pl.when(lat_ok(step))
        def _():
            weight_copy(step).start()

    def send_local(number, _):
        which, chunk = jnp.where(number < CHUNKS, early, 1 - early), number % CHUNKS
        for step in (-1, 1):

            @pl.when(lat_ok(step))
            def _():
                local_copy(which, chunk, step).start()

        return 0

    lax.fori_loop(0, 2 * CHUNKS, send_local, 0)

    for copy in raw_loads:
        copy.wait()

    def prepare(g, _):
        for k in range(9):
            flipped = jnp.transpose(raw[g, k])
            lead = flipped.astype(jnp.bfloat16)
            here = slice(k * TILE, (k + 1) * TILE)
            high[g, here, :] = lead
            low[g, here, :] = (flipped - lead.astype(jnp.float32)).astype(jnp.bfloat16)
        return 0

    lax.fori_loop(0, tiles, prepare, 0)

    for step in (-1, 1):

        @pl.when(lat_ok(step))
        def _():
            weight_copy(step).wait_send()

    for step in (-1, 1):

        @pl.when(lat_ok(-step))
        def _():
            weight_copy(step).wait_recv()

    def run(number, _):
        which, chunk = event(number)
        has_in = depth_ok(2 * which - 1)
        has_out = depth_ok(1 - 2 * which)
        sign = (1 - 2 * which).astype(jnp.float32)
        for step in (-1, 1):

            @pl.when(lat_ok(-step))
            def _():
                local_copy(which, chunk, step).wait_recv()

        for step in (0, -1, 1):

            @pl.when(has_in & lat_ok(-step))
            def _():
                field_copy(which, chunk, step).wait_recv()

        for slot in range(3):
            scale = 1.0 + sign * weight[slot]
            scale = jnp.concatenate([scale, scale], axis=0)
            field = local[which, chunk, slot] + scale * arrived[which, chunk, slot]
            lead = field.astype(jnp.bfloat16)
            here = slice(slot * width, (slot + 1) * width)
            split[:ROWS, here] = lead
            split[ROWS:, here] = (field - lead.astype(jnp.float32)).astype(jnp.bfloat16)
        for g in range(tiles):
            start = (g + 1 + shift[0, g]) * TILE
            window = split[:, pl.ds(start, 9 * TILE)]
            both = jnp.dot(window, high[g], preferred_element_type=jnp.float32)
            rest = jnp.dot(window[:ROWS], low[g], preferred_element_type=jnp.float32)
            total = both[:ROWS] + both[ROWS:] + rest
            here = slice(g * TILE, (g + 1) * TILE)
            result[which, chunk, :GROUP, here] = total[:GROUP, :TILE] - total[GROUP:, TILE:]
            result[which, chunk, GROUP:, here] = total[GROUP:, :TILE] + total[:GROUP, TILE:]
        for step in (0, -1, 1):

            @pl.when(has_out & lat_ok(step))
            def _():
                field_copy(which, chunk, step).start()

        return 0

    lax.fori_loop(0, 2 * CHUNKS, run, 0)

    for which, out in ((DOWN, down_out), (UP, up_out)):
        for g in range(tiles):
            here = slice(g * TILE, (g + 1) * TILE)
            groups = [None] * (2 * CHUNKS)
            for chunk in range(CHUNKS):
                for part in range(2):
                    groups[column_group(chunk, part)] = result[
                        which, chunk, part * GROUP : (part + 1) * GROUP, here
                    ]
            out[here, :] = jnp.transpose(jnp.concatenate(groups, axis=0))

    def finish(number, _):
        which, chunk = number // CHUNKS, number % CHUNKS
        for step in (-1, 1):

            @pl.when(lat_ok(step))
            def _():
                local_copy(which, chunk, step).wait_send()

        for step in (0, -1, 1):

            @pl.when(depth_ok(1 - 2 * which) & lat_ok(step))
            def _():
                field_copy(which, chunk, step).wait_send()

        return 0

    lax.fori_loop(0, 2 * CHUNKS, finish, 0)


def solution(mesh):
    sections = mesh.shape["depth"]
    lat_devices = mesh.shape["lat"]

    def shards(operator, band_shift, reflectivity, up_stored, down_stored, sources, assignment):
        tiles = operator.shape[1]
        width = tiles * TILE
        anywhere = pl.BlockSpec(memory_space=pl.ANY)
        in_vmem = pl.BlockSpec(memory_space=pltpu.VMEM)
        in_smem = pl.BlockSpec(memory_space=pltpu.SMEM)
        dma = pltpu.SemaphoreType.DMA

        def body(*refs):
            kernel(sections, lat_devices, *refs)

        down, up = pl.pallas_call(
            body,
            out_shape=[jax.ShapeDtypeStruct((width, COLS), jnp.float32)] * 2,
            in_specs=[anywhere, in_smem, in_vmem, anywhere, anywhere, anywhere, in_smem],
            out_specs=[in_vmem, in_vmem],
            scratch_shapes=[
                pltpu.VMEM((tiles, 9, 2 * TILE, TILE), jnp.float32),
                pltpu.VMEM((tiles, 9 * TILE, 2 * TILE), jnp.bfloat16),
                pltpu.VMEM((tiles, 9 * TILE, 2 * TILE), jnp.bfloat16),
                pltpu.VMEM((width, COLS), jnp.float32),
                pltpu.VMEM((width, COLS), jnp.float32),
                pltpu.VMEM((width, COLS), jnp.float32),
                pltpu.VMEM((2, CHUNKS, 3, ROWS, width), jnp.float32),
                pltpu.VMEM((3, 8, width), jnp.float32),
                pltpu.VMEM((2, CHUNKS, 3, ROWS, width), jnp.float32),
                pltpu.VMEM((2, CHUNKS, ROWS, width), jnp.float32),
                pltpu.VMEM((2 * ROWS, 3 * width), jnp.bfloat16),
                dma((3,)),
                dma((tiles,)),
                dma((2, CHUNKS, 3)),
                dma((2, CHUNKS, 3)),
                dma((3,)),
                dma((3,)),
                dma((2, CHUNKS, 3)),
                dma((2, CHUNKS, 3)),
            ],
            compiler_params=pltpu.CompilerParams(
                collective_id=0, has_side_effects=True, vmem_limit_bytes=60 * 2**20
            ),
            name="round_trip",
        )(operator, band_shift, reflectivity, up_stored, down_stored, sources, assignment)
        return down[None], up[None]

    return jax.shard_map(
        shards,
        mesh=mesh,
        in_specs=(
            P("depth", "lat", None, None, None),
            P("depth", "lat"),
            P("depth", "lat"),
            P("depth", "lat", None),
            P("depth", "lat", None),
            P("lat", None),
            P(),
        ),
        out_specs=(P("depth", "lat", None), P("depth", "lat", None)),
        check_vma=False,
    )
```

profile of v0, /device:TPU:99, one launch (start us, length us, event | category | flops | bytes accessed | tf_op | source)
XLA Modules:
  0.0 97.4 jit_solution(2008954243523100188)
XLA Ops:
  0.6 93.3 %round_trip.1 = (f32[640,128]{1,0:T(8,128)}, f32[640,128]{1,0:T(8,128)}) custom-call(f32[1,5,9,256,128]{4,3,2,1,0:T(8,128)} %refs_0_.1, s32[1,5]{1,0:T(1,128)} %refs_1_.1, f32[1,640]{1,0:T(1,128)} %refs_2_.1, f32[1,640,128]{2,1,0:T(8,128)} %refs_3_.1, f32[1,640,128]{2,1,0:T(8,128)} %refs_4_.1, f32[640,128]{1,0:T(8,128)} %refs_5_.1, s32[64]{0:T(128)} %refs_6_.1), custom_call_target="tpu_custom_call" | custom-call | tf_op jit(solution)/shard_map/round_trip/pallas_call | solution.py:343
  93.9 1.7 %copy.11 = f32[1,640,128]{2,1,0:T(8,128)} copy(f32[1,640,128]{2,1,0:T(8,128)} %bitcast.3) | data formatting | bytes 655360
  95.6 1.7 %copy.12 = f32[1,640,128]{2,1,0:T(8,128)} copy(f32[1,640,128]{2,1,0:T(8,128)} %bitcast.2) | data formatting | bytes 655360
where the time goes:
time: 99.2 us; the launch traced here: 97.4 us
  Pallas kernels  93.3 us (94%)
  local copies, waits for them, and re-layouts  3.44 us (3%)
    pallas_call x1, Pallas kernels, shards(): pl.pallas_call(body, out_shape=[jax.ShapeDtypeStruct((width, COLS), jnp.f...  93.3 us
    unnamed x2, local copies, waits for them, and re-layouts  3.44 us

commit v1 on v0

--- a/solution.py
+++ b/solution.py
@@ -30,23 +30,24 @@
     down_stored,
     sources,
     assignment,
-    down_out,
-    up_out,
+    result,
     raw,
     high,
     low,
     up_rows,
     down_rows,
     source_rows,
+    mine,
     local,
     weight,
+    terms,
     arrived,
-    result,
+    leaving,
     split,
     load_sem,
     raw_sem,
-    local_send,
-    local_recv,
+    term_send,
+    term_recv,
     weight_send,
     weight_recv,
     field_send,
@@ -100,23 +101,22 @@
                 )
 
     strength = reflect[...]
-    weight[1] = jnp.broadcast_to(strength, (8, width))
-
-    def put_local(which, rows, scale, offset=None):
+    mine[...] = jnp.broadcast_to(strength, mine.shape)
+
+    def pieces(rows):
         for g in range(tiles):
             flipped = jnp.transpose(rows[g * TILE : (g + 1) * TILE, :])
             here = slice(g * TILE, (g + 1) * TILE)
             for chunk in range(CHUNKS):
                 for part in range(2):
                     group = column_group(chunk, part)
-                    value = flipped[group * GROUP : (group + 1) * GROUP] * scale[:, here]
-                    if offset is not None:
-                        value = value + local[which, chunk, 1, part * GROUP : (part + 1) * GROUP, here]
-                    local[which, chunk, 1, part * GROUP : (part + 1) * GROUP, here] = value
+                    place = slice(part * GROUP, (part + 1) * GROUP)
+                    yield chunk, place, here, flipped[group * GROUP : (group + 1) * GROUP]
 
     loads[0].wait()
     loads[1].wait()
-    put_local(DOWN, up_rows[...], -strength)
+    for chunk, place, here, value in pieces(up_rows[...]):
+        local[DOWN, chunk, place, here] = -strength[:, here] * value
 
     @pl.when(depth == 0)
     def _():
@@ -133,25 +133,26 @@
             precision=lax.Precision.HIGHEST,
             preferred_element_type=jnp.float32,
         )
-        put_local(DOWN, entering, 1.0 + strength, offset=True)
-        arrived[DOWN] = jnp.zeros(arrived.shape[1:], jnp.float32)
+        for chunk, place, here, value in pieces(entering):
+            arrived[DOWN, chunk, 1, place, here] = (
+                local[DOWN, chunk, place, here] + (1.0 + strength[:, here]) * value
+            )
 
     loads[2].wait()
-    put_local(UP, down_rows[...], strength)
+    for chunk, place, here, value in pieces(down_rows[...]):
+        local[UP, chunk, place, here] = strength[:, here] * value
 
     @pl.when(depth == sections - 1)
     def _():
-        arrived[UP] = jnp.zeros(arrived.shape[1:], jnp.float32)
+        for chunk in range(CHUNKS):
+            arrived[UP, chunk, 1] = local[UP, chunk]
 
     for edge, slot in ((0, 0), (lat_devices - 1, 2)):
 
         @pl.when(lat == edge)
         def _():
-            weight[slot] = jnp.zeros(weight.shape[1:], jnp.float32)
-
             def clear(which, _):
                 for chunk in range(CHUNKS):
-                    local[which, chunk, slot] = jnp.zeros((ROWS, width), jnp.float32)
                     arrived[which, chunk, slot] = jnp.zeros((ROWS, width), jnp.float32)
                 return 0
 
@@ -159,24 +160,34 @@
 
     pl.semaphore_wait(barrier, greeted)
 
-    def weight_copy(step):
+    def term_copy(which, half):
+        some = pl.ds(half * (CHUNKS // 2), CHUNKS // 2)
+        return pltpu.make_async_remote_copy(
+            src_ref=local.at[which, some],
+            dst_ref=terms.at[which, some],
+            send_sem=term_send.at[which, half],
+            recv_sem=term_recv.at[which, half],
+            device_id=(depth - 1 + 2 * which, lat),
+            device_id_type=MESH,
+        )
+
+    def weight_copy(which):
+        return pltpu.make_async_remote_copy(
+            src_ref=mine,
+            dst_ref=weight.at[which],
+            send_sem=weight_send.at[which],
+            recv_sem=weight_recv.at[which],
+            device_id=(depth - 1 + 2 * which, lat),
+            device_id_type=MESH,
+        )
+
+    def first_copy(which, chunk, step):
         slot = 1 - step
         return pltpu.make_async_remote_copy(
-            src_ref=weight.at[1],
-            dst_ref=weight.at[slot],
-            send_sem=weight_send.at[slot],
-            recv_sem=weight_recv.at[slot],
-            device_id=(depth, lat + step),
-            device_id_type=MESH,
-        )
-
-    def local_copy(which, chunk, step):
-        slot = 1 - step
-        return pltpu.make_async_remote_copy(
-            src_ref=local.at[which, chunk, 1],
-            dst_ref=local.at[which, chunk, slot],
-            send_sem=local_send.at[which, chunk, slot],
-            recv_sem=local_recv.at[which, chunk, slot],
+            src_ref=arrived.at[which, chunk, 1],
+            dst_ref=arrived.at[which, chunk, slot],
+            send_sem=field_send.at[1 - which, chunk, slot],
+            recv_sem=field_recv.at[which, chunk, slot],
             device_id=(depth, lat + step),
             device_id_type=MESH,
         )
@@ -184,7 +195,7 @@
     def field_copy(which, chunk, step):
         slot = 1 - step
         return pltpu.make_async_remote_copy(
-            src_ref=result.at[which, chunk],
+            src_ref=leaving.at[which, chunk],
             dst_ref=arrived.at[which, chunk, slot],
             send_sem=field_send.at[which, chunk, slot],
             recv_sem=field_recv.at[which, chunk, slot],
@@ -207,23 +218,33 @@
         )
         return jnp.where(of_early, early, 1 - early), chunk
 
-    for step in (-1, 1):
-
-        @pl.when(lat_ok(step))
-        def _():
-            weight_copy(step).start()
-
-    def send_local(number, _):
-        which, chunk = jnp.where(number < CHUNKS, early, 1 - early), number % CHUNKS
-        for step in (-1, 1):
-
-            @pl.when(lat_ok(step))
+    at_end = (depth == 0) | (depth == sections - 1)
+
+    @pl.when(at_end)
+    def _():
+        def send_first(chunk, _):
+            for step in (-1, 1):
+
+                @pl.when(lat_ok(step))
+                def _():
+                    first_copy(early, chunk, step).start()
+
+            return 0
+
+        lax.fori_loop(0, CHUNKS, send_first, 0)
+
+    for which in (DOWN, UP):
+
+        @pl.when(depth_ok(2 * which - 1))
+        def _():
+            weight_copy(which).start()
+
+    for half in range(2):
+        for which in (DOWN, UP):
+
+            @pl.when(depth_ok(2 * which - 1))
             def _():
-                local_copy(which, chunk, step).start()
-
-        return 0
-
-    lax.fori_loop(0, 2 * CHUNKS, send_local, 0)
+                term_copy(which, half).start()
 
     for copy in raw_loads:
         copy.wait()
@@ -239,43 +260,39 @@
 
     lax.fori_loop(0, tiles, prepare, 0)
 
-    for step in (-1, 1):
-
-        @pl.when(lat_ok(step))
-        def _():
-            weight_copy(step).wait_send()
-
-    for step in (-1, 1):
-
-        @pl.when(lat_ok(-step))
-        def _():
-            weight_copy(step).wait_recv()
+    for which in (DOWN, UP):
+
+        @pl.when(depth_ok(1 - 2 * which))
+        def _():
+            weight_copy(which).wait_recv()
 
     def run(number, _):
         which, chunk = event(number)
         has_in = depth_ok(2 * which - 1)
         has_out = depth_ok(1 - 2 * which)
         sign = (1 - 2 * which).astype(jnp.float32)
+
+        @pl.when(has_in)
+        def _():
+            field_copy(which, chunk, 0).wait_recv()
+
         for step in (-1, 1):
 
             @pl.when(lat_ok(-step))
             def _():
-                local_copy(which, chunk, step).wait_recv()
-
-        for step in (0, -1, 1):
-
-            @pl.when(has_in & lat_ok(-step))
-            def _():
                 field_copy(which, chunk, step).wait_recv()
 
         for slot in range(3):
-            scale = 1.0 + sign * weight[slot]
-            scale = jnp.concatenate([scale, scale], axis=0)
-            field = local[which, chunk, slot] + scale * arrived[which, chunk, slot]
+            field = arrived[which, chunk, slot]
             lead = field.astype(jnp.bfloat16)
             here = slice(slot * width, (slot + 1) * width)
             split[:ROWS, here] = lead
             split[ROWS:, here] = (field - lead.astype(jnp.float32)).astype(jnp.bfloat16)
+
+        @pl.when(has_out & (chunk % (CHUNKS // 2) == 0))
+        def _():
+            term_copy(which, chunk // (CHUNKS // 2)).wait_recv()
+
         for g in range(tiles):
             start = (g + 1 + shift[0, g]) * TILE
             window = split[:, pl.ds(start, 9 * TILE)]
@@ -285,6 +302,13 @@
             here = slice(g * TILE, (g + 1) * TILE)
             result[which, chunk, :GROUP, here] = total[:GROUP, :TILE] - total[GROUP:, TILE:]
             result[which, chunk, GROUP:, here] = total[GROUP:, :TILE] + total[:GROUP, TILE:]
+
+        @pl.when(has_out)
+        def _():
+            scale = 1.0 + sign * weight[which]
+            scale = jnp.concatenate([scale, scale], axis=0)
+            leaving[which, chunk] = terms[which, chunk] + scale * result[which, chunk]
+
         for step in (0, -1, 1):
 
             @pl.when(has_out & lat_ok(step))
@@ -295,8 +319,43 @@
 
     lax.fori_loop(0, 2 * CHUNKS, run, 0)
 
+    for which in (DOWN, UP):
+
+        @pl.when(depth_ok(2 * which - 1))
+        def _():
+            weight_copy(which).wait_send()
+            for half in range(2):
+                term_copy(which, half).wait_send()
+
+    @pl.when(at_end)
+    def _():
+        def finish_first(chunk, _):
+            for step in (-1, 1):
+
+                @pl.when(lat_ok(step))
+                def _():
+                    first_copy(early, chunk, step).wait_send()
+
+            return 0
+
+        lax.fori_loop(0, CHUNKS, finish_first, 0)
+
+    def finish(number, _):
+        which, chunk = number // CHUNKS, number % CHUNKS
+        for step in (0, -1, 1):
+
+            @pl.when(depth_ok(1 - 2 * which) & lat_ok(step))
+            def _():
+                field_copy(which, chunk, step).wait_send()
+
+        return 0
+
+    lax.fori_loop(0, 2 * CHUNKS, finish, 0)
+
+
+def unpack(result, down_out, up_out):
     for which, out in ((DOWN, down_out), (UP, up_out)):
-        for g in range(tiles):
+        for g in range(out.shape[0] // TILE):
             here = slice(g * TILE, (g + 1) * TILE)
             groups = [None] * (2 * CHUNKS)
             for chunk in range(CHUNKS):
@@ -306,24 +365,6 @@
                     ]
             out[here, :] = jnp.transpose(jnp.concatenate(groups, axis=0))
 
-    def finish(number, _):
-        which, chunk = number // CHUNKS, number % CHUNKS
-        for step in (-1, 1):
-
-            @pl.when(lat_ok(step))
-            def _():
-                local_copy(which, chunk, step).wait_send()
-
-        for step in (0, -1, 1):
-
-            @pl.when(depth_ok(1 - 2 * which) & lat_ok(step))
-            def _():
-                field_copy(which, chunk, step).wait_send()
-
-        return 0
-
-    lax.fori_loop(0, 2 * CHUNKS, finish, 0)
-
 
 def solution(mesh):
     sections = mesh.shape["depth"]
@@ -340,11 +381,11 @@
         def body(*refs):
             kernel(sections, lat_devices, *refs)
 
-        down, up = pl.pallas_call(
+        result = pl.pallas_call(
             body,
-            out_shape=[jax.ShapeDtypeStruct((width, COLS), jnp.float32)] * 2,
+            out_shape=jax.ShapeDtypeStruct((2, CHUNKS, ROWS, width), jnp.float32),
             in_specs=[anywhere, in_smem, in_vmem, anywhere, anywhere, anywhere, in_smem],
-            out_specs=[in_vmem, in_vmem],
+            out_specs=in_vmem,
             scratch_shapes=[
                 pltpu.VMEM((tiles, 9, 2 * TILE, TILE), jnp.float32),
                 pltpu.VMEM((tiles, 9 * TILE, 2 * TILE), jnp.bfloat16),
@@ -352,17 +393,19 @@
                 pltpu.VMEM((width, COLS), jnp.float32),
                 pltpu.VMEM((width, COLS), jnp.float32),
                 pltpu.VMEM((width, COLS), jnp.float32),
-                pltpu.VMEM((2, CHUNKS, 3, ROWS, width), jnp.float32),
-                pltpu.VMEM((3, 8, width), jnp.float32),
+                pltpu.VMEM((8, width), jnp.float32),
+                pltpu.VMEM((2, CHUNKS, ROWS, width), jnp.float32),
+                pltpu.VMEM((2, 8, width), jnp.float32),
+                pltpu.VMEM((2, CHUNKS, ROWS, width), jnp.float32),
                 pltpu.VMEM((2, CHUNKS, 3, ROWS, width), jnp.float32),
                 pltpu.VMEM((2, CHUNKS, ROWS, width), jnp.float32),
                 pltpu.VMEM((2 * ROWS, 3 * width), jnp.bfloat16),
                 dma((3,)),
                 dma((tiles,)),
-                dma((2, CHUNKS, 3)),
-                dma((2, CHUNKS, 3)),
-                dma((3,)),
-                dma((3,)),
+                dma((2, 2)),
+                dma((2, 2)),
+                dma((2,)),
+                dma((2,)),
                 dma((2, CHUNKS, 3)),
                 dma((2, CHUNKS, 3)),
             ],
@@ -371,6 +414,13 @@
             ),
             name="round_trip",
         )(operator, band_shift, reflectivity, up_stored, down_stored, sources, assignment)
+        down, up = pl.pallas_call(
+            unpack,
+            out_shape=[jax.ShapeDtypeStruct((width, COLS), jnp.float32)] * 2,
+            in_specs=[in_vmem],
+            out_specs=[in_vmem, in_vmem],
+            name="unpack",
+        )(result)
         return down[None], up[None]
 
     return jax.shard_map(

time: 99.2 us -> 90.9 us (0.916); the launches traced: 97.4 us -> 90.7 us
  local copies, waits for them, and re-layouts: 3.44 us -> 0 us
  Pallas kernels: 93.3 us -> 90.1 us
    unnamed x2 -> x0, local copies, waits for them, and re-layouts: 3.44 us -> none
    pallas_call x1 -> x2, Pallas kernels: 93.3 us -> 90.1 us  [the longest x1 88 us: shards(): pl.pallas_call(body, out_shape=jax.ShapeDtypeStruct((2, CHUNKS, ROWS, wid...]
where the time goes in v1:
time: 90.9 us; the launch traced here: 90.7 us
  Pallas kernels  90.1 us (99%)
    pallas_call x1, Pallas kernels, shards(): pl.pallas_call(body, out_shape=jax.ShapeDtypeStruct((2, CHUNKS, ROWS, wid...  88 us
    pallas_call x1, Pallas kernels, shards(): pl.pallas_call(unpack, out_shape=[jax.ShapeDtypeStruct((width, COLS), jnp...  2.09 us

profile of v1, /device:TPU:99, one launch (start us, length us, event | category | flops | bytes accessed | tf_op | source)
XLA Modules:
  0.0 90.7 jit_solution(16296843661228783578)
XLA Ops:
  0.6 88.0 %round_trip.1.result = f32[2,8,16,640]{3,2,1,0:T(8,128)} custom-call(f32[1,5,9,256,128]{4,3,2,1,0:T(8,128)} %refs_0_.1, s32[1,5]{1,0:T(1,128)} %refs_1_.1, f32[1,640]{1,0:T(1,128)} %refs_2_.1, f32[1,640,128]{2,1,0:T(8,128)} %refs_3_.1, f32[1,640,128]{2,1,0:T(8,128)} %refs_4_.1, f32[640,128]{1,0:T(8,128)} %refs_5_.1, s32[64]{0:T(128)} %refs_6_.1), custom_call_target="tpu_custom_call" | custom-call | tf_op jit(solution)/shard_map/round_trip/pallas_call | solution.py:384
  88.6 2.1 %unpack.1 = (f32[640,128]{1,0:T(8,128)}, f32[640,128]{1,0:T(8,128)}) custom-call(f32[2,8,16,640]{3,2,1,0:T(8,128)} %round_trip.1.result), custom_call_target="tpu_custom_call" | custom-call | tf_op jit(solution)/shard_map/unpack/pallas_call | solution.py:417

commit v2 on v1

--- a/solution.py
+++ b/solution.py
@@ -13,6 +13,7 @@
 PER_BATCH = SHOTS // GROUP
 COLS = 4 * SHOTS
 DOWN, UP = 0, 1
+WINDOW = 2
 MESH = pl.DeviceIdType.MESH
 
 
@@ -231,7 +232,7 @@
 
             return 0
 
-        lax.fori_loop(0, CHUNKS, send_first, 0)
+        lax.fori_loop(0, 1, send_first, 0)
 
     for which in (DOWN, UP):
 
@@ -268,6 +269,15 @@
 
     def run(number, _):
         which, chunk = event(number)
+
+        @pl.when(at_end & (which == early) & (chunk + 1 < CHUNKS))
+        def _():
+            for step in (-1, 1):
+
+                @pl.when(lat_ok(step))
+                def _():
+                    first_copy(early, chunk + 1, step).start()
+
         has_in = depth_ok(2 * which - 1)
         has_out = depth_ok(1 - 2 * which)
         sign = (1 - 2 * which).astype(jnp.float32)
@@ -311,6 +321,12 @@
 
         for step in (0, -1, 1):
 
+            @pl.when(has_out & lat_ok(step) & (chunk >= WINDOW))
+            def _():
+                field_copy(which, chunk - WINDOW, step).wait_send()
+
+        for step in (0, -1, 1):
+
             @pl.when(has_out & lat_ok(step))
             def _():
                 field_copy(which, chunk, step).start()
@@ -344,7 +360,7 @@
         which, chunk = number // CHUNKS, number % CHUNKS
         for step in (0, -1, 1):
 
-            @pl.when(depth_ok(1 - 2 * which) & lat_ok(step))
+            @pl.when(depth_ok(1 - 2 * which) & lat_ok(step) & (chunk >= CHUNKS - WINDOW))
             def _():
                 field_copy(which, chunk, step).wait_send()
 

time: 90.9 us -> 81.6 us (0.90); the launches traced: 90.7 us -> 80.4 us
  Pallas kernels: 90.1 us -> 79.7 us
    pallas_call x1, Pallas kernels: 88 us -> 77.7 us  [shards(): pl.pallas_call(body, out_shape=jax.ShapeDtypeStruct((2, CHUNKS, ROWS, wid...]
where the time goes in v2:
time: 81.6 us; the launch traced here: 80.4 us
  Pallas kernels  79.7 us (98%)
    pallas_call x1, Pallas kernels, shards(): pl.pallas_call(body, out_shape=jax.ShapeDtypeStruct((2, CHUNKS, ROWS, wid...  77.7 us
    pallas_call x1, Pallas kernels, shards(): pl.pallas_call(unpack, out_shape=[jax.ShapeDtypeStruct((width, COLS), jnp...  2.09 us

profile of v2, /device:TPU:99, one launch (start us, length us, event | category | flops | bytes accessed | tf_op | source)
XLA Modules:
  0.0 80.4 jit_solution(4793908204076946294)
XLA Ops:
  0.6 77.7 %round_trip.1.result = f32[2,8,16,640]{3,2,1,0:T(8,128)} custom-call(f32[1,5,9,256,128]{4,3,2,1,0:T(8,128)} %refs_0_.1, s32[1,5]{1,0:T(1,128)} %refs_1_.1, f32[1,640]{1,0:T(1,128)} %refs_2_.1, f32[1,640,128]{2,1,0:T(8,128)} %refs_3_.1, f32[1,640,128]{2,1,0:T(8,128)} %refs_4_.1, f32[640,128]{1,0:T(8,128)} %refs_5_.1, s32[64]{0:T(128)} %refs_6_.1), custom_call_target="tpu_custom_call" | custom-call | tf_op jit(solution)/shard_map/round_trip/pallas_call | solution.py:400
  78.3 2.1 %unpack.1 = (f32[640,128]{1,0:T(8,128)}, f32[640,128]{1,0:T(8,128)}) custom-call(f32[2,8,16,640]{3,2,1,0:T(8,128)} %round_trip.1.result), custom_call_target="tpu_custom_call" | custom-call | tf_op jit(solution)/shard_map/unpack/pallas_call | solution.py:433

commit v3 on v1

--- a/solution.py
+++ b/solution.py
@@ -13,6 +13,7 @@
 PER_BATCH = SHOTS // GROUP
 COLS = 4 * SHOTS
 DOWN, UP = 0, 1
+WINDOW = 2
 MESH = pl.DeviceIdType.MESH
 
 
@@ -52,6 +53,7 @@
     weight_recv,
     field_send,
     field_recv,
+    share_send,
 ):
     depth = lax.axis_index("depth")
     lat = lax.axis_index("lat")
@@ -192,31 +194,36 @@
             device_id_type=MESH,
         )
 
-    def field_copy(which, chunk, step):
+    def field_copy(which, chunk, step, piece=pl.ds(0, width)):
         slot = 1 - step
         return pltpu.make_async_remote_copy(
-            src_ref=leaving.at[which, chunk],
-            dst_ref=arrived.at[which, chunk, slot],
+            src_ref=leaving.at[which, chunk, :, piece],
+            dst_ref=arrived.at[which, chunk, slot, :, piece],
             send_sem=field_send.at[which, chunk, slot],
             recv_sem=field_recv.at[which, chunk, slot],
             device_id=(depth + 1 - 2 * which, lat + step),
             device_id_type=MESH,
         )
 
+    def shares(section):
+        return (section < sections // 2 - 1) | (section > sections // 2)
+
+    inner = 1 - 2 * (lat % 2)
+    outer = -inner
+
+    def share_copy(which, chunk, arriving=False):
+        slot = 1 + inner if arriving else 1 - inner
+        return pltpu.make_async_remote_copy(
+            src_ref=arrived.at[which, chunk, 1],
+            dst_ref=arrived.at[which, chunk, slot],
+            send_sem=share_send.at[which, chunk],
+            recv_sem=field_recv.at[which, chunk, slot],
+            device_id=(depth, lat + inner),
+            device_id_type=MESH,
+        )
+
     early = jnp.where(2 * depth < sections, DOWN, UP)
     lag = jnp.where((depth == sections // 2 - 1) | (depth == sections // 2), 3, CHUNKS)
-
-    def event(number):
-        mixed = (number >= lag) & (number < 2 * CHUNKS - lag)
-        turn = (number - lag) // 2
-        odd = (number - lag) % 2
-        of_early = (number < lag) | (mixed & (odd == 1))
-        chunk = jnp.where(
-            number < lag,
-            number,
-            jnp.where(mixed, jnp.where(odd == 1, lag + turn, turn), number - CHUNKS),
-        )
-        return jnp.where(of_early, early, 1 - early), chunk
 
     at_end = (depth == 0) | (depth == sections - 1)
 
@@ -231,7 +238,7 @@
 
             return 0
 
-        lax.fori_loop(0, CHUNKS, send_first, 0)
+        lax.fori_loop(0, 1, send_first, 0)
 
     for which in (DOWN, UP):
 
@@ -266,54 +273,106 @@
         def _():
             weight_copy(which).wait_recv()
 
-    def run(number, _):
-        which, chunk = event(number)
-        has_in = depth_ok(2 * which - 1)
-        has_out = depth_ok(1 - 2 * which)
-        sign = (1 - 2 * which).astype(jnp.float32)
-
-        @pl.when(has_in)
-        def _():
-            field_copy(which, chunk, 0).wait_recv()
-
-        for step in (-1, 1):
-
-            @pl.when(lat_ok(-step))
-            def _():
-                field_copy(which, chunk, step).wait_recv()
-
-        for slot in range(3):
-            field = arrived[which, chunk, slot]
-            lead = field.astype(jnp.bfloat16)
-            here = slice(slot * width, (slot + 1) * width)
-            split[:ROWS, here] = lead
-            split[ROWS:, here] = (field - lead.astype(jnp.float32)).astype(jnp.bfloat16)
-
-        @pl.when(has_out & (chunk % (CHUNKS // 2) == 0))
-        def _():
-            term_copy(which, chunk // (CHUNKS // 2)).wait_recv()
-
+    split_at = (tiles + 1) // 2
+
+    def process(items):
+        count = len(items)
+        for which, chunk in items:
+            has_in = depth_ok(2 * which - 1)
+
+            @pl.when(has_in)
+            def _():
+                field_copy(which, chunk, 0).wait_recv()
+
+            @pl.when(has_in & shares(depth))
+            def _():
+                share_copy(which, chunk).start()
+
+        for n, (which, chunk) in enumerate(items):
+            share_copy(which, chunk, arriving=True).wait_recv()
+
+            @pl.when(lat_ok(outer))
+            def _():
+                field_copy(which, chunk, -outer).wait_recv()
+
+            @pl.when(depth_ok(1 - 2 * which) & (chunk % (CHUNKS // 2) == 0))
+            def _():
+                term_copy(which, chunk // (CHUNKS // 2)).wait_recv()
+
+            leads = slice(n * ROWS, (n + 1) * ROWS)
+            rests = slice((count + n) * ROWS, (count + n + 1) * ROWS)
+            for slot in range(3):
+                field = arrived[which, chunk, slot]
+                lead = field.astype(jnp.bfloat16)
+                here = slice(slot * width, (slot + 1) * width)
+                split[leads, here] = lead
+                split[rests, here] = (field - lead.astype(jnp.float32)).astype(jnp.bfloat16)
+
+        def leave(first, last):
+            piece = pl.ds(first * TILE, (last - first) * TILE)
+            for which, chunk in items:
+                has_out = depth_ok(1 - 2 * which)
+                sign = (1 - 2 * which).astype(jnp.float32)
+
+                @pl.when(has_out)
+                def _():
+                    scale = 1.0 + sign * weight[which, :, piece]
+                    scale = jnp.concatenate([scale, scale], axis=0)
+                    leaving[which, chunk, :, piece] = (
+                        terms[which, chunk, :, piece] + scale * result[which, chunk, :, piece]
+                    )
+
+                direct = jnp.logical_not(shares(depth + 1 - 2 * which))
+                ways = ((0, True), (inner, direct), (outer, True))
+                if first == 0:
+                    for step, used in ways:
+
+                        @pl.when(has_out & lat_ok(step) & used & (chunk >= WINDOW))
+                        def _():
+                            field_copy(which, chunk - WINDOW, step).wait_send()
+
+                for step, used in ways:
+
+                    @pl.when(has_out & lat_ok(step) & used)
+                    def _():
+                        field_copy(which, chunk, step, piece).start()
+
+        half = count * ROWS
         for g in range(tiles):
             start = (g + 1 + shift[0, g]) * TILE
-            window = split[:, pl.ds(start, 9 * TILE)]
+            window = split[: 2 * half, pl.ds(start, 9 * TILE)]
             both = jnp.dot(window, high[g], preferred_element_type=jnp.float32)
-            rest = jnp.dot(window[:ROWS], low[g], preferred_element_type=jnp.float32)
-            total = both[:ROWS] + both[ROWS:] + rest
+            rest = jnp.dot(window[:half], low[g], preferred_element_type=jnp.float32)
+            total = both[:half] + both[half:] + rest
             here = slice(g * TILE, (g + 1) * TILE)
-            result[which, chunk, :GROUP, here] = total[:GROUP, :TILE] - total[GROUP:, TILE:]
-            result[which, chunk, GROUP:, here] = total[GROUP:, :TILE] + total[:GROUP, TILE:]
-
-        @pl.when(has_out)
-        def _():
-            scale = 1.0 + sign * weight[which]
-            scale = jnp.concatenate([scale, scale], axis=0)
-            leaving[which, chunk] = terms[which, chunk] + scale * result[which, chunk]
-
-        for step in (0, -1, 1):
-
-            @pl.when(has_out & lat_ok(step))
-            def _():
-                field_copy(which, chunk, step).start()
+            for n, (which, chunk) in enumerate(items):
+                real = total[n * ROWS : n * ROWS + GROUP]
+                imag = total[n * ROWS + GROUP : (n + 1) * ROWS]
+                result[which, chunk, :GROUP, here] = real[:, :TILE] - imag[:, TILE:]
+                result[which, chunk, GROUP:, here] = imag[:, :TILE] + real[:, TILE:]
+            if g + 1 in (split_at, tiles):
+                leave(0 if g + 1 == split_at else split_at, g + 1)
+
+
+    def run(number, _):
+        @pl.when(at_end & (number + 1 < CHUNKS))
+        def _():
+            for step in (-1, 1):
+
+                @pl.when(lat_ok(step))
+                def _():
+                    first_copy(early, number + 1, step).start()
+
+        paired = (number >= lag) & (number < CHUNKS)
+
+        @pl.when(paired)
+        def _():
+            process([(early, number), (1 - early, number - lag)])
+
+        @pl.when(jnp.logical_not(paired) & (number < CHUNKS + lag))
+        def _():
+            begun = number < lag
+            process([(jnp.where(begun, early, 1 - early), jnp.where(begun, number, number - lag))])
 
         return 0
 
@@ -342,9 +401,15 @@
 
     def finish(number, _):
         which, chunk = number // CHUNKS, number % CHUNKS
-        for step in (0, -1, 1):
-
-            @pl.when(depth_ok(1 - 2 * which) & lat_ok(step))
+
+        @pl.when(depth_ok(2 * which - 1) & shares(depth))
+        def _():
+            share_copy(which, chunk).wait_send()
+
+        direct = jnp.logical_not(shares(depth + 1 - 2 * which))
+        for step, used in ((0, True), (inner, direct), (outer, True)):
+
+            @pl.when(depth_ok(1 - 2 * which) & lat_ok(step) & used & (chunk >= CHUNKS - WINDOW))
             def _():
                 field_copy(which, chunk, step).wait_send()
 
@@ -399,7 +464,7 @@
                 pltpu.VMEM((2, CHUNKS, ROWS, width), jnp.float32),
                 pltpu.VMEM((2, CHUNKS, 3, ROWS, width), jnp.float32),
                 pltpu.VMEM((2, CHUNKS, ROWS, width), jnp.float32),
-                pltpu.VMEM((2 * ROWS, 3 * width), jnp.bfloat16),
+                pltpu.VMEM((4 * ROWS, 3 * width), jnp.bfloat16),
                 dma((3,)),
                 dma((tiles,)),
                 dma((2, 2)),
@@ -408,6 +473,7 @@
                 dma((2,)),
                 dma((2, CHUNKS, 3)),
                 dma((2, CHUNKS, 3)),
+                dma((2, CHUNKS)),
             ],
             compiler_params=pltpu.CompilerParams(
                 collective_id=0, has_side_effects=True, vmem_limit_bytes=60 * 2**20

time: 90.9 us -> 79.8 us (0.88)
  Pallas kernels: 90.1 us -> 79.1 us
    pallas_call x1, Pallas kernels: 88 us -> 77 us  [shards(): pl.pallas_call(body, out_shape=jax.ShapeDtypeStruct((2, CHUNKS, ROWS, wid...]
where the time goes in v3:
time: 79.8 us; the launch traced here: 79.7 us
  Pallas kernels  79.1 us (99%)
    pallas_call x1, Pallas kernels, shards(): pl.pallas_call(body, out_shape=jax.ShapeDtypeStruct((2, CHUNKS, ROWS, wid...  77 us
    pallas_call x1, Pallas kernels, shards(): pl.pallas_call(unpack, out_shape=[jax.ShapeDtypeStruct((width, COLS), jnp...  2.09 us

profile of v3, /device:TPU:99, one launch (start us, length us, event | category | flops | bytes accessed | tf_op | source)
XLA Modules:
  0.0 79.7 jit_solution(11694385028452886079)
XLA Ops:
  0.6 77.0 %round_trip.1.result = f32[2,8,16,640]{3,2,1,0:T(8,128)} custom-call(f32[1,5,9,256,128]{4,3,2,1,0:T(8,128)} %refs_0_.1, s32[1,5]{1,0:T(1,128)} %refs_1_.1, f32[1,640]{1,0:T(1,128)} %refs_2_.1, f32[1,640,128]{2,1,0:T(8,128)} %refs_3_.1, f32[1,640,128]{2,1,0:T(8,128)} %refs_4_.1, f32[640,128]{1,0:T(8,128)} %refs_5_.1, s32[64]{0:T(128)} %refs_6_.1), custom_call_target="tpu_custom_call" | custom-call | tf_op jit(solution)/shard_map/round_trip/pallas_call | solution.py:449
  77.6 2.1 %unpack.1 = (f32[640,128]{1,0:T(8,128)}, f32[640,128]{1,0:T(8,128)}) custom-call(f32[2,8,16,640]{3,2,1,0:T(8,128)} %round_trip.1.result), custom_call_target="tpu_custom_call" | custom-call | tf_op jit(solution)/shard_map/unpack/pallas_call | solution.py:483

commit v4 on v3

--- a/solution.py
+++ b/solution.py
@@ -418,17 +418,38 @@
     lax.fori_loop(0, 2 * CHUNKS, finish, 0)
 
 
-def unpack(result, down_out, up_out):
-    for which, out in ((DOWN, down_out), (UP, up_out)):
-        for g in range(out.shape[0] // TILE):
-            here = slice(g * TILE, (g + 1) * TILE)
-            groups = [None] * (2 * CHUNKS)
-            for chunk in range(CHUNKS):
-                for part in range(2):
-                    groups[column_group(chunk, part)] = result[
-                        which, chunk, part * GROUP : (part + 1) * GROUP, here
-                    ]
-            out[here, :] = jnp.transpose(jnp.concatenate(groups, axis=0))
+def unpack(result, down_out, up_out, held, turned, in_sem, out_sem):
+    outs = (down_out, up_out)
+    tiles = down_out.shape[0] // TILE
+
+    def load(which, g):
+        here = pl.ds(g * TILE, TILE)
+        return pltpu.make_async_copy(
+            result.at[which, :, :, here], held.at[which, :, :, here], in_sem.at[which, g]
+        )
+
+    def store(which, g):
+        here = pl.ds(g * TILE, TILE)
+        return pltpu.make_async_copy(
+            turned.at[which, here], outs[which].at[here], out_sem.at[which, g]
+        )
+
+    order = [(which, g) for which in (DOWN, UP) for g in range(tiles)]
+    for which, g in order:
+        load(which, g).start()
+    for which, g in order:
+        load(which, g).wait()
+        here = slice(g * TILE, (g + 1) * TILE)
+        groups = [None] * (2 * CHUNKS)
+        for chunk in range(CHUNKS):
+            for part in range(2):
+                groups[column_group(chunk, part)] = held[
+                    which, chunk, part * GROUP : (part + 1) * GROUP, here
+                ]
+        turned[which, here, :] = jnp.transpose(jnp.concatenate(groups, axis=0))
+        store(which, g).start()
+    for which, g in order:
+        store(which, g).wait()
 
 
 def solution(mesh):
@@ -483,8 +504,15 @@
         down, up = pl.pallas_call(
             unpack,
             out_shape=[jax.ShapeDtypeStruct((width, COLS), jnp.float32)] * 2,
-            in_specs=[in_vmem],
-            out_specs=[in_vmem, in_vmem],
+            in_specs=[anywhere],
+            out_specs=[anywhere, anywhere],
+            scratch_shapes=[
+                pltpu.VMEM((2, CHUNKS, ROWS, width), jnp.float32),
+                pltpu.VMEM((2, width, COLS), jnp.float32),
+                dma((2, tiles)),
+                dma((2, tiles)),
+            ],
+            compiler_params=pltpu.CompilerParams(vmem_limit_bytes=60 * 2**20),
             name="unpack",
         )(result)
         return down[None], up[None]

time: 79.8 us -> 80.7 us (1.011)
  no operation moved by 1% of the time
where the time goes in v4:
time: 80.7 us; the launch traced here: 80.4 us
  Pallas kernels  79.8 us (99%)
    pallas_call x1, Pallas kernels, shards(): pl.pallas_call(body, out_shape=jax.ShapeDtypeStruct((2, CHUNKS, ROWS, wid...  77.1 us
    pallas_call x1, Pallas kernels, shards(): pl.pallas_call(unpack, out_shape=[jax.ShapeDtypeStruct((width, COLS), jnp...  2.66 us

profile of v4, /device:TPU:99, one launch (start us, length us, event | category | flops | bytes accessed | tf_op | source)
XLA Modules:
  0.0 80.4 jit_solution(14919728674850368336)
XLA Ops:
  0.6 77.1 %round_trip.1.result = f32[2,8,16,640]{3,2,1,0:T(8,128)} custom-call(f32[1,5,9,256,128]{4,3,2,1,0:T(8,128)} %refs_0_.1, s32[1,5]{1,0:T(1,128)} %refs_1_.1, f32[1,640]{1,0:T(1,128)} %refs_2_.1, f32[1,640,128]{2,1,0:T(8,128)} %refs_3_.1, f32[1,640,128]{2,1,0:T(8,128)} %refs_4_.1, f32[640,128]{1,0:T(8,128)} %refs_5_.1, s32[64]{0:T(128)} %refs_6_.1), custom_call_target="tpu_custom_call" | custom-call | tf_op jit(solution)/shard_map/round_trip/pallas_call | solution.py:470
  77.8 2.7 %unpack.1 = (f32[640,128]{1,0:T(8,128)}, f32[640,128]{1,0:T(8,128)}) custom-call(f32[2,8,16,640]{3,2,1,0:T(8,128)} %round_trip.1.result), custom_call_target="tpu_custom_call" | custom-call | tf_op jit(solution)/shard_map/unpack/pallas_call | solution.py:504
